TPU v7x, 128 devices: a whole 4x4x4 slice. The times are simulated.
128 devices in a mesh: grp: 4 (over z), aux: 32 (over y, x, core).
Axes of the slice: x: 4, y: 4, z: 4, core: 2. Of those that a mesh axis runs over, the one named last changes fastest.
Arguments:
- three_index: bfloat16 [64, 768, 16384], P(None, None, ('grp', 'aux')), may hold values from -0.25 to 0.25
- block_owner: int32 [64], replicated, may hold values from 0 to 31, as said below
- pair_screen: int32 [64, 64], replicated, may hold values from 0 to 1, as said below
- orbital_counts: int32 [64], replicated, may hold values from 1 to 16, as said below
- occupied_energy: float32 [64, 16], replicated, may hold values from -1.5 to -0.3
- virtual_energy: float32 [64, 48], replicated, may hold values from 0.3 to 2.5
Outputs:
- virtual_density: float32 [64, 48, 48], P('aux', 'grp')
Inputs may be any that keep to these rules, and one draw needn't show every extreme that they name: `block_owner`: every owner index holds 1 to 3 blocks, and some hold exactly 3. `pair_screen`: symmetric, with ones on the diagonal. `orbital_counts`: some block uses all 16 slots.
All inputs are finite; a program needn't handle non-finite values.
Results may differ from a plain program's by a relative error of at most 0.0019.
Values may be sent and summed in bfloat16 or wider, within the bound.
A program may use at most 128 MiB of HBM per device.

v0:
```python
import jax
import jax.numpy as jnp
from jax import lax
from jax.experimental import pallas as pl
from jax.experimental.pallas import tpu as pltpu
from jax.sharding import PartitionSpec as P

CAP = 3


def slot_tiles(source, slot_block, slot_valid, owners):
    picked = jnp.take(source, slot_block.reshape(-1), axis=0)
    picked = picked.reshape(owners, CAP, source.shape[1], source.shape[2])
    return jnp.where(slot_valid[:, :, None, None] > 0, picked, jnp.zeros_like(picked))


def pair_block(received, first, second):
    return lax.dot_general(
        lax.dynamic_index_in_dim(received, first, 1, False),
        lax.dynamic_index_in_dim(received, second, 1, False),
        (((0, 2), (0, 2)), ((), ())),
        preferred_element_type=jnp.float32,
    )


def general(three_index, block_owner, pair_screen, orbital_counts, occupied_energy, virtual_energy):
    block_count, row_count, aux_local = three_index.shape
    occupied_width = occupied_energy.shape[1]
    virtual_width = virtual_energy.shape[1]
    groups = lax.axis_size("grp")
    owners = lax.axis_size("aux")
    own_index = lax.axis_index("aux")
    group_index = lax.axis_index("grp")
    quarter = row_count // groups
    owner_ids = jnp.arange(owners, dtype=jnp.int32)
    owned = (block_owner[None, :] == owner_ids[:, None]).astype(jnp.int32)
    slot_rank = jnp.cumsum(owned, axis=1) - 1
    slot_ids = jnp.arange(CAP, dtype=jnp.int32)
    selection = owned[:, None, :] * (slot_rank[:, None, :] == slot_ids[None, :, None]).astype(
        jnp.int32
    )
    block_ids = jnp.arange(block_count, dtype=jnp.int32)
    slot_block = jnp.sum(selection * block_ids[None, None, :], axis=2)
    slot_valid = jnp.sum(selection, axis=2)
    mine = lax.dynamic_index_in_dim(selection, own_index, 0, keepdims=False)
    my_block = jnp.sum(mine * block_ids[None, :], axis=1)
    my_valid = jnp.sum(mine, axis=1)
    energy = (virtual_energy[:, None, :] - occupied_energy[:, :, None]).reshape(
        block_count, row_count
    )
    occupied_flags = (
        jnp.arange(occupied_width, dtype=jnp.int32)[None, :] < orbital_counts[:, None]
    ).astype(jnp.float32)
    occupancy = jnp.repeat(occupied_flags, virtual_width, axis=1)
    slot_energy = jnp.take(energy, my_block, axis=0)
    slot_occupancy = jnp.take(occupancy, my_block, axis=0)
    screened = jnp.take(jnp.take(pair_screen, my_block, axis=0), my_block, axis=1)
    is_live = screened * my_valid[:, None] * my_valid[None, :] > 0

    def slot_amplitude(integral, first, second):
        energy_rows = lax.dynamic_slice_in_dim(slot_energy[first], group_index * quarter, quarter)
        occupied_rows = lax.dynamic_slice_in_dim(
            slot_occupancy[first], group_index * quarter, quarter
        )
        divisor = energy_rows[:, None] + slot_energy[second][None, :]
        return (
            occupied_rows[:, None] * slot_occupancy[second][None, :] * integral / divisor
        ).astype(jnp.bfloat16)

    def own_density(amplitude):
        row_form = amplitude.reshape(quarter // virtual_width, virtual_width, row_count)
        return jnp.einsum("iax,ibx->ab", row_form, row_form, preferred_element_type=jnp.float32)

    outgoing = slot_tiles(three_index, slot_block, slot_valid, owners)
    received = lax.all_to_all(outgoing, "aux", split_axis=0, concat_axis=0, tiled=True)
    empty = jnp.zeros((virtual_width, virtual_width), jnp.float32)

    def one_pair(parts, pair):
        first = pair // CAP
        second = pair % CAP
        integral = pair_block(received, first, second)
        sent = integral.reshape(groups, quarter, row_count)
        summed = jnp.sum(lax.all_to_all(sent, "grp", 0, 0, tiled=True), axis=0)
        part = own_density(slot_amplitude(summed, first, second))
        part = jnp.where(is_live[first, second], part, empty)
        return parts.at[first].add(part), None

    slot_parts, _ = lax.scan(
        one_pair,
        jnp.zeros((CAP, virtual_width, virtual_width), jnp.float32),
        jnp.arange(CAP * CAP, dtype=jnp.int32),
    )
    spread = slot_parts.reshape(CAP, groups, virtual_width // groups, virtual_width)
    placed = jnp.einsum(
        "cb,cgxy->gbxy", mine.astype(jnp.float32), spread, precision=lax.Precision.HIGHEST
    )
    placed = placed.reshape(groups, owners, block_count // owners, virtual_width // groups, virtual_width)
    placed = jnp.sum(lax.all_to_all(placed, "grp", 0, 0, tiled=True), axis=0)
    return jnp.sum(lax.all_to_all(placed, "aux", 0, 0, tiled=True), axis=0)


NV = 48
OB = 16
BINS = 16
GROUP = 8
ROWS = GROUP * NV
SIDE = 4
PART_A = 6
PART_B = 2
GROUPS = PART_A + PART_B
SLOTS = GROUPS * GROUP
CHUNK = 16
ALL = (0, BINS)
LIMITS = (ALL, ALL, ALL, (0, 15), (0, 9), (0, 4), ALL, (2, BINS))
STREAMS = tuple((GROUP * k, GROUP, ALL) for k in range(5)) + (
    (40, 4, ALL),
    (44, 4, (0, 8)),
    (48, 4, (0, 4)),
)
SENT = 52
AHEAD = 2
COLUMNS = tuple(
    [(0, v, v * (v + 1) // 2) for v in range(PART_A)]
    + [(PART_A, v, PART_A * (PART_A + 1) // 2 + v * (v + 1) // 2) for v in range(PART_B)]
)
TILES = PART_A * (PART_A + 1) // 2 + PART_B * (PART_B + 1) // 2
UNITS = []
for column, (base, v, first) in enumerate(COLUMNS):
    for skip in range(0, v + 1, 2):
        turn = len(UNITS) % 3
        UNITS.append(
            (column, first + skip, min(2, v + 1 - skip), (turn, (turn + 1) % 3, (turn + 2) % 3))
        )
BITS = [(d % 2, (d // 2) % 2, d // 4) for d in range(8)]
MESH = pl.DeviceIdType.MESH
VMEM = pl.BlockSpec(memory_space=pltpu.VMEM)
SMEM = pl.BlockSpec(memory_space=pltpu.SMEM)
ANY = pl.BlockSpec(memory_space=pl.ANY)


def has(limits, index):
    first, end = limits
    return (index >= first) & (index < end)


def plan(block_owner, orbital_counts):
    ids = jnp.arange(block_owner.shape[0], dtype=jnp.int32)
    same = block_owner[:, None] == block_owner[None, :]
    earlier = same & (ids[None, :] < ids[:, None])
    load = jnp.sum(jnp.where(same, orbital_counts[None, :], 0), axis=1)
    base = jnp.sum(jnp.where(earlier, orbital_counts[None, :], 0), axis=1)
    place = jnp.sum(earlier.astype(jnp.int32), axis=1)
    ahead = (load[None, :] > load[:, None]) | (
        (load[None, :] == load[:, None]) & (block_owner[None, :] < block_owner[:, None])
    )
    rank = jnp.sum((ahead & (place == 0)[None, :]).astype(jnp.int32), axis=1)
    second = rank >= BINS
    bin_of = jnp.where(second, 2 * BINS - 1 - rank, rank)
    ahead_load = jnp.sum(
        jnp.where(
            (place == 0)[None, :] & (rank[None, :] == 2 * BINS - 1 - rank[:, None]), load[None, :], 0
        ),
        axis=1,
    )
    room = jnp.zeros_like(load)
    for group, limits in enumerate(LIMITS):
        room = room + jnp.where(second == (group >= PART_A), has(limits, bin_of) * GROUP, 0)
    sent = sum(has(limits, bin_of) * number for first, number, limits in STREAMS)
    fits = jnp.all((load <= room) & (load + ahead_load <= sent))
    return bin_of, base, jnp.where(second, ahead_load, 0), load, place, second, fits


def position():
    z = lax.axis_index("grp")
    aux = lax.axis_index("aux")
    core = lax.rem(aux, 2)
    x = lax.rem(aux // 2, SIDE)
    y = aux // (2 * SIDE)
    return x, y, z, core


def device(x, y, z, core):
    return (z, (y * SIDE + x) * 2 + core)


def bin_index(x, y, z, core):
    kind = lax.rem(x, 2) + 2 * lax.rem(y, 2) + 4 * lax.rem(z, 2)
    return kind + core * (BINS - 1 - 2 * kind)


def part_index(x, y, z):
    return x // 2 + 2 * (y // 2) + 4 * (z // 2)


def shifted(value, by):
    return lax.rem(value + by + SIDE, SIDE)


def kernel(
    origin_ref,
    meta_ref,
    source,
    meta,
    screen,
    occupied_energy,
    virtual_energy,
    out,
    whole,
    packed,
    held,
    tiles,
    parts_1,
    parts_2,
    parts_3,
    exact,
    exact_parts,
    stack,
    row_sums,
    slot_sums,
    fold,
    chunks,
    chunk_parts,
    dense,
    homes,
    row_energy,
    column_energy,
    mask,
    load_sem,
    local_sem,
    send_sem,
    recv_sem,
    tile_send,
    tile_recv,
    exact_send,
    exact_recv,
    chunk_send,
    chunk_recv,
    home_send,
    home_recv,
):
    x, y, z, core = position()
    aux = lax.axis_index("aux")
    owners = lax.axis_size("aux")
    sign = 1 - 2 * core
    own_bin = bin_index(x, y, z, core)
    own_part = part_index(x, y, z)
    quarter = lax.rem(own_part, SIDE)
    half = own_part // SIDE

    pieces = load_sem.shape[0]
    size = source.shape[0] // pieces

    def load(piece):
        part = pl.ds(piece * size, size)
        return pltpu.make_async_copy(source.at[part], whole.at[part], load_sem.at[piece])

    for piece in range(pieces):
        load(piece).start()

    barrier = pltpu.get_barrier_semaphore()

    def greet(target):
        pl.semaphore_signal(barrier, inc=1, device_id=target, device_id_type=MESH)

    greet(device(x, y, z, 1 - core))
    for d in range(1, 8):
        dx, dy, dz = BITS[d]
        greet(device(shifted(x, -dx), shifted(y, -dy), shifted(z, -dz), 0))
        greet(device(shifted(x, dx), shifted(y, dy), shifted(z, dz), 1))
        greet(device(shifted(x, 2 * dx), shifted(y, 2 * dy), shifted(z, 2 * dz), core))

    def feeder(index):
        number = index // 2
        feed_core = number // 8
        kind = number + feed_core * (BINS - 1 - 2 * number)
        return (
            lax.rem(kind, 2) + 2 * lax.rem(z, 2),
            lax.rem(kind // 2, 2) + 2 * (z // 2),
            kind // 4 + 2 * lax.rem(index, 2),
            feed_core,
        )

    own_feed = own_bin * 2 + half

    @pl.loop(0, owners)
    def _(index):
        @pl.when((quarter != z) | (index != own_feed))
        def _():
            greet(device(*feeder(index)))

    fold[...] = (
        lax.rem(lax.broadcasted_iota(jnp.int32, (ROWS, NV), 0), NV)
        == lax.broadcasted_iota(jnp.int32, (ROWS, NV), 1)
    ).astype(jnp.float32)
    slot_sums[...] = jnp.zeros_like(slot_sums)
    row_sums[...] = jnp.zeros_like(row_sums)
    chunks[...] = jnp.zeros_like(chunks)

    for piece in range(pieces):
        load(piece).wait()
    pl.semaphore_wait(barrier, 22 + owners - (quarter == z).astype(jnp.int32))

    def when(limits, index, act):
        if limits == ALL:
            act()
        else:
            pl.when(has(limits, index))(act)

    def slots(stream):
        first, number, limits = STREAMS[stream]
        return pl.ds(first, number)

    def gather(d, target_core, stream, act):
        dx, dy, dz = d % 2, (d // 2) % 2, d // 4
        tx, ty, tz = shifted(x, sign * dx), shifted(y, sign * dy), shifted(z, sign * dz)
        target_bin = bin_index(tx, ty, tz, target_core)
        copy = pltpu.make_async_remote_copy(
            src_ref=packed.at[target_bin, slots(stream)],
            dst_ref=held.at[2 * d + core, slots(stream)],
            send_sem=send_sem.at[2 * d + target_core, stream],
            recv_sem=recv_sem.at[2 * d + core, stream],
            device_id=device(tx, ty, tz, target_core),
            device_id_type=MESH,
        )
        when(STREAMS[stream][2], target_bin, lambda: act(copy))

    def keep(stream):
        return pltpu.make_async_copy(
            packed.at[own_bin, slots(stream)], held.at[core, slots(stream)], local_sem.at[stream]
        )

    def send_stream(stream):
        first_slot, number_of_slots, limits = STREAMS[stream]

        @pl.loop(0, BINS)
        def _(number):
            for slot in range(first_slot, first_slot + number_of_slots):
                origin = origin_ref[number * SENT + slot]
                packed[number, slot] = whole[origin]

        @pl.loop(0, 14)
        def _(index):
            gather(7 - index // 2, lax.rem(index, 2), stream, lambda copy: copy.start())

        gather(0, 1 - core, stream, lambda copy: copy.start())
        when(limits, own_bin, lambda: keep(stream).start())

    for stream in range(AHEAD):
        send_stream(stream)

    def arrived(stream):
        def wait_all():
            keep(stream).wait()

            @pl.loop(2, BINS)
            def _(sender):
                part = held.at[sender, slots(stream)]
                pltpu.make_async_copy(part, part, recv_sem.at[sender, stream]).wait()

            part = held.at[1 - core, slots(stream)]
            pltpu.make_async_copy(part, part, recv_sem.at[1 - core, stream]).wait()

        when(STREAMS[stream][2], own_bin, wait_all)

    row_number = lax.broadcasted_iota(jnp.int32, (ROWS, ROWS), 0)
    column_number = lax.broadcasted_iota(jnp.int32, (ROWS, ROWS), 1)
    own_diagonal = (
        lax.broadcasted_iota(jnp.int32, (NV, ROWS), 0) + own_part * NV
        == lax.broadcasted_iota(jnp.int32, (NV, ROWS), 1)
    )
    same_slot = (
        lax.broadcasted_iota(jnp.int32, (GROUP, ROWS), 1) // NV
        == lax.broadcasted_iota(jnp.int32, (GROUP, ROWS), 0)
    )

    def exact_dot(left, right, axis=0):
        return lax.dot_general(
            left,
            right,
            (((1,), (axis,)), ((), ())),
            precision=lax.Precision.HIGHEST,
            preferred_element_type=jnp.float32,
        )

    blocks = meta.shape[1]
    slot_number = lax.broadcasted_iota(jnp.int32, (SLOTS, blocks), 0)
    orbital = slot_number - meta[1:2, :]
    inside = (meta[0:1, :] == own_bin) & (orbital >= 0) & (orbital < meta[2:3, :])
    pick = jnp.where(inside, 1.0, 0.0)
    slot_orbital = jnp.sum(jnp.where(inside, orbital, 0), axis=1, keepdims=True)
    occupied = exact_dot(pick, occupied_energy[...], 1)
    occupied = jnp.where(
        lax.broadcasted_iota(jnp.int32, (SLOTS, OB), 1) == slot_orbital, occupied, 0.0
    )
    energy = exact_dot(pick, virtual_energy[...], 1) - jnp.sum(occupied, axis=1, keepdims=True)
    row_slot = lax.broadcasted_iota(jnp.int32, (GROUPS, SLOTS), 0) * GROUP + own_part
    column_slot = lax.broadcasted_iota(jnp.int32, (GROUPS, SLOTS), 1)
    row_pick = exact_dot(jnp.where(row_slot == column_slot, 1.0, 0.0), pick)
    live = exact_dot(exact_dot(row_pick, jnp.where(screen[...] == 1, 1.0, 0.0)), pick, 1)
    order = jnp.where(row_slot < column_slot, 2.0, jnp.where(row_slot == column_slot, 1.0, 0.0))
    kind = jnp.where(live > 0.5, order, 0.0)
    for group in range(GROUPS):
        lanes = exact_dot(energy[group * GROUP : (group + 1) * GROUP], fold[...], 1)
        lanes = jnp.sum(jnp.where(same_slot, lanes, 0.0), axis=0, keepdims=True)
        column_energy[group] = lanes
        row_energy[group] = jnp.sum(jnp.where(own_diagonal, lanes, 0.0), axis=1, keepdims=True)
        wide = lax.broadcasted_iota(jnp.int32, (SLOTS, ROWS), 0) == (
            group * GROUP + lax.broadcasted_iota(jnp.int32, (SLOTS, ROWS), 1) // NV
        )
        mask[group] = exact_dot(kind, jnp.where(wide, 1.0, 0.0))

    def find(block, found):
        result = []
        for index in range(6):
            hit = (
                (meta_ref[0, block] == own_bin)
                & (meta_ref[3, block] == index % 3)
                & (meta_ref[4, block] == index // 3)
            )
            old = found[3 * index : 3 * index + 3]
            new = (meta_ref[1, block], meta_ref[2, block], block)
            result += [jnp.where(hit, n, o) for n, o in zip(new, old)]
        return tuple(result)

    nothing = jnp.int32(0)
    found = lax.fori_loop(0, blocks, find, (nothing, nothing, jnp.int32(-1)) * 6)
    block_start, block_slots, block_id = found[0::3], found[1::3], found[2::3]

    def settle():
        offset = block_slots[0] + block_slots[1] + block_slots[2]

        @pl.loop(0, BINS)
        def _(sender):
            for slot in range(PART_B * GROUP):
                held[sender, SENT + slot] = held[sender, offset + slot]

    def rows_of(base, group):
        first = group * GROUP + (SENT if base else 0)
        return jnp.concatenate(
            [
                held[sender, pl.ds(first, GROUP)].reshape(ROWS, held.shape[-1])
                for sender in range(BINS)
            ],
            axis=1,
        )

    def peer(e):
        dx, dy, dz = BITS[e]
        px, py, pz = shifted(x, 2 * dx), shifted(y, 2 * dy), shifted(z, 2 * dz)
        return part_index(px, py, pz), device(px, py, pz, core)

    bit = (x // 2, y // 2, z // 2)

    def view(fixed):
        return tuple(fixed.get(axis, slice(None)) for axis in (2, 1, 0))

    def step(unit, phase):
        column, first, number, order = UNITS[unit]
        fixed = {axis: bit[axis] for axis in order[:phase]}
        axis = order[phase]
        fixed[axis] = 1 - bit[axis]
        run = pl.ds(first, number)
        far = [shifted(c, 2 * (axis == k)) for k, c in enumerate((x, y, z))]
        landing = (parts_1.at[:, :, run], parts_2.at[:, run], parts_3.at[run])[phase]
        return pltpu.make_async_remote_copy(
            src_ref=tiles.at[view(fixed) + (run,)],
            dst_ref=landing,
            send_sem=tile_send.at[unit, phase],
            recv_sem=tile_recv.at[unit, phase],
            device_id=device(*far, core),
            device_id_type=MESH,
        )

    def units_of(column):
        return [unit for unit in range(len(UNITS)) if UNITS[unit][0] == column]

    def merge(column, phase):
        for unit in units_of(column):
            _, first, number, order = UNITS[unit]
            step(unit, phase).wait_recv()
            fixed = {axis: bit[axis] for axis in order[: phase + 1]}
            rest = [axis for axis in (2, 1, 0) if axis not in fixed]
            landed = (parts_1, parts_2)[phase]

            @pl.loop(first, first + number)
            def _(index):
                for choice in range(2 ** len(rest)):
                    at = tuple((choice // 2**k) % 2 for k in range(len(rest)))
                    place = view({**fixed, **dict(zip(rest, at))}) + (index,)
                    tiles[place] = (
                        tiles[place].astype(jnp.float32) + landed[at + (index,)].astype(jnp.float32)
                    ).astype(jnp.bfloat16)

            step(unit, phase + 1).start()

    def scatter_exact(e, batch):
        part, target = peer(e)
        return pltpu.make_async_remote_copy(
            src_ref=exact.at[batch, part],
            dst_ref=exact_parts.at[e - 1, batch],
            send_sem=exact_send.at[e - 1, batch],
            recv_sem=exact_recv.at[e - 1, batch],
            device_id=target,
            device_id_type=MESH,
        )

    def make_column(column):
        base, v, first = COLUMNS[column]

        @pl.loop(0, v + 1)
        def _(u):
            tile = lax.dot_general(
                rows_of(base, u),
                rows_of(base, v),
                (((1,), (1,)), ((), ())),
                preferred_element_type=jnp.float32,
            )

            @pl.when(u == v)
            def _():
                diagonal = jnp.where(row_number == column_number, tile, 0.0)
                diagonal = jnp.where(same_slot, jnp.sum(diagonal, axis=0, keepdims=True), 0.0)
                diagonal = exact_dot(diagonal, fold[...])
                for part in range(8):
                    exact[column // 4, part, column % 4 : column % 4 + 1, :NV] = diagonal[
                        part : part + 1
                    ]

            rounded = tile.astype(jnp.bfloat16)
            for part in range(8):
                tiles[part // 4, (part // 2) % 2, part % 2, first + u] = rounded[
                    part * NV : (part + 1) * NV
                ]

        for unit in units_of(column):
            step(unit, 0).start()

    def add_column(column):
        base, v, first = COLUMNS[column]
        for unit in units_of(column):
            step(unit, 2).wait_recv()
        diagonal = exact[column // 4, own_part]
        for e in range(7):
            diagonal = diagonal + exact_parts[e, column // 4]
        diagonal = exact_dot(diagonal[:, :NV], fold[...], 1)[column % 4 : column % 4 + 1]

        @pl.loop(0, v + 1)
        def _(u):
            integral = tiles[bit[2], bit[1], bit[0], first + u].astype(jnp.float32) + parts_3[
                first + u
            ].astype(jnp.float32)
            integral = jnp.where(own_diagonal & (u == v), diagonal, integral)
            kind = mask[base + v, pl.ds(base + u, 1), :]
            quotient = integral / (row_energy[base + u] + column_energy[base + v])
            amplitude = jnp.where(kind > 0, quotient, 0.0).astype(jnp.bfloat16)
            row_sums[base + u] = row_sums[base + u] + lax.dot_general(
                amplitude, amplitude, (((1,), (1,)), ((), ())), preferred_element_type=jnp.float32
            )
            stack[pl.ds(pl.multiple_of(u * NV, NV), NV), :] = jnp.where(
                kind > 1, quotient, 0.0
            ).astype(jnp.bfloat16)

        stacked = stack[: (v + 1) * NV, :]
        product = lax.dot_general(
            stacked, stacked, (((0,), (0,)), ((), ())), preferred_element_type=jnp.float32
        )
        slot_sums[(base + v) * ROWS : (base + v + 1) * ROWS, :] = jnp.dot(
            jnp.where(row_number // NV == column_number // NV, product, 0.0),
            fold[...],
            precision=lax.Precision.HIGHEST,
            preferred_element_type=jnp.float32,
        )

    def advance(column, phase):
        if column < 0:
            return
        act = (
            lambda: make_column(column),
            lambda: merge(column, 0),
            lambda: merge(column, 1),
            lambda: add_column(column),
        )[phase]
        when(LIMITS[column], own_bin, act)

    def receive(stream):
        arrived(stream)
        if stream + AHEAD < len(STREAMS):
            send_stream(stream + AHEAD)

    def start_exact(batch):
        for e in range(7, 0, -1):
            scatter_exact(e, batch).start()

    def wait_exact(batch):
        for e in range(1, 8):
            scatter_exact(e, batch).wait_recv()

    for column in range(PART_A):
        receive(column)
        if column == PART_A - 1:
            receive(PART_A)
        advance(column, 0)
        if column == 3:
            start_exact(0)
        advance(column - 1, 1)
        advance(column - 2, 2)
        if column == 3:
            wait_exact(0)
        advance(column - 3, 3)
    receive(len(STREAMS) - 1)
    settle()
    late = range(PART_A, GROUPS)
    for column in late:
        advance(column, 0)
    start_exact(1)
    for column in (PART_A - 1, *late):
        advance(column, 1)
    advance(PART_A - 2, 2)
    advance(PART_A - 3, 3)
    for column in (PART_A - 1, *late):
        advance(column, 2)
    wait_exact(1)
    for column in (PART_A - 2, PART_A - 1, *late):
        advance(column, 3)
    for group in range(GROUPS):
        part = pl.ds(pl.multiple_of(group * ROWS + own_part * NV, NV), NV)
        slot_sums[part, :] = slot_sums[part, :] + row_sums[group]

    for side in range(2):
        first_slot = side * PART_A * GROUP

        def add_slot(step, sums):
            slot = first_slot + step
            value = slot_sums[pl.ds(pl.multiple_of(slot * NV, NV), NV), :]
            result = []
            for i in range(3 * side, 3 * side + 3):
                own = (slot >= block_start[i]) & (slot < block_start[i] + block_slots[i])
                result.append(sums[i % 3] + jnp.where(own, value, jnp.zeros_like(value)))
            return tuple(result)

        zero = jnp.zeros((NV, NV), jnp.float32)
        sums = lax.fori_loop(0, (PART_A, PART_B)[side] * GROUP, add_slot, (zero, zero, zero))
        width = NV // SIDE
        for i in range(3):
            for g in range(SIDE):
                chunks[side * SIDE + g, i * CHUNK : i * CHUNK + width, :NV] = sums[i][
                    g * width : (g + 1) * width
                ]

    def scatter_chunk(e):
        part, target = peer(e)
        return pltpu.make_async_remote_copy(
            src_ref=chunks.at[part],
            dst_ref=chunk_parts.at[e - 1],
            send_sem=chunk_send.at[e - 1],
            recv_sem=chunk_recv.at[e - 1],
            device_id=target,
            device_id_type=MESH,
        )

    for e in range(7, 0, -1):
        scatter_chunk(e).start()
    for e in range(1, 8):
        scatter_chunk(e).wait_recv()
    total = chunks[own_part]
    for e in range(7):
        total = total + chunk_parts[e]
    pieces = [total[i * CHUNK : (i + 1) * CHUNK] for i in range(3)]
    turned = [pltpu.roll(piece, 64, 1) for piece in pieces]

    def send_home(target):
        return pltpu.make_async_remote_copy(
            src_ref=dense.at[target],
            dst_ref=homes.at[own_feed],
            send_sem=home_send.at[target],
            recv_sem=home_recv.at[own_feed],
            device_id=(quarter, target),
            device_id_type=MESH,
        )

    def away(target):
        return (quarter != z) | (target != aux)

    @pl.loop(0, owners)
    def _(target):
        message = jnp.zeros((CHUNK, 128), jnp.float32)
        for i in range(3):
            block = jnp.where(half == 0, block_id[i], block_id[3 + i])
            message = message + jnp.where(block == 2 * target, pieces[i], 0.0)
            message = message + jnp.where(block == 2 * target + 1, turned[i], 0.0)
        dense[target] = message

        @pl.when(away(target))
        def _():
            send_home(target).start()

    @pl.when(quarter == z)
    def _():
        homes[own_feed] = dense[aux]

    @pl.loop(0, owners)
    def _(index):
        @pl.when((quarter != z) | (index != own_feed))
        def _():
            pltpu.make_async_copy(homes.at[index], homes.at[index], home_recv.at[index]).wait()

    out[...] = jnp.sum(homes[...], axis=0)

    @pl.loop(0, owners)
    def _(target):
        @pl.when(away(target))
        def _():
            send_home(target).wait_send()

    for e in range(1, 8):
        scatter_chunk(e).wait_send()

    def sent_column(column):
        for unit in units_of(column):
            for phase in range(3):
                step(unit, phase).wait_send()

    for column in range(GROUPS):
        when(LIMITS[column], own_bin, lambda: sent_column(column))
    for batch in range(2):
        for e in range(1, 8):
            scatter_exact(e, batch).wait_send()
    for stream in range(len(STREAMS)):
        gather(0, 1 - core, stream, lambda copy: copy.wait_send())

        @pl.loop(2, BINS)
        def _(index):
            gather(index // 2, lax.rem(index, 2), stream, lambda copy: copy.wait_send())


def binned(
    bin_of,
    base,
    offset,
    load,
    place,
    second,
    three_index,
    block_owner,
    pair_screen,
    orbital_counts,
    occupied_energy,
    virtual_energy,
):
    blocks, row_count, aux_local = three_index.shape
    block_ids = jnp.arange(blocks, dtype=jnp.int32)
    sent_ids = jnp.arange(SENT, dtype=jnp.int32)[:, None] - (base + offset)[None, :]
    bins = jnp.arange(BINS, dtype=jnp.int32)
    origin = jnp.sum(
        jnp.where(
            (bin_of[None, None, :] == bins[:, None, None])
            & ((sent_ids >= 0) & (sent_ids < orbital_counts[None, :]))[None],
            (block_ids[None, :] * OB + sent_ids)[None],
            0,
        ),
        axis=2,
    )
    start = base + jnp.where(second, PART_A * GROUP, 0)
    meta = jnp.stack([bin_of, start, orbital_counts, place, second.astype(jnp.int32)] + [base] * 3)
    owners = lax.axis_size("aux")
    home = pl.pallas_call(
        kernel,
        out_shape=jax.ShapeDtypeStruct((CHUNK, 128), jnp.float32),
        in_specs=[SMEM, SMEM, ANY, VMEM, VMEM, VMEM, VMEM],
        out_specs=VMEM,
        scratch_shapes=[
            pltpu.VMEM((blocks * OB, NV, aux_local), jnp.bfloat16),
            pltpu.VMEM((BINS, SENT, NV, aux_local), jnp.bfloat16),
            pltpu.VMEM((BINS, SENT + PART_B * GROUP, NV, aux_local), jnp.bfloat16),
            pltpu.VMEM((2, 2, 2, TILES, NV, ROWS), jnp.bfloat16),
            pltpu.VMEM((2, 2, TILES, NV, ROWS), jnp.bfloat16),
            pltpu.VMEM((2, TILES, NV, ROWS), jnp.bfloat16),
            pltpu.VMEM((TILES, NV, ROWS), jnp.bfloat16),
            pltpu.VMEM((2, 8, 8, 128), jnp.float32),
            pltpu.VMEM((7, 2, 8, 128), jnp.float32),
            pltpu.VMEM((PART_A * NV, ROWS), jnp.bfloat16),
            pltpu.VMEM((GROUPS, NV, NV), jnp.float32),
            pltpu.VMEM((SLOTS * NV, NV), jnp.float32),
            pltpu.VMEM((ROWS, NV), jnp.float32),
            pltpu.VMEM((8, 3 * CHUNK, 128), jnp.float32),
            pltpu.VMEM((7, 3 * CHUNK, 128), jnp.float32),
            pltpu.VMEM((owners, CHUNK, 128), jnp.float32),
            pltpu.VMEM((owners, CHUNK, 128), jnp.float32),
            pltpu.VMEM((GROUPS, NV, 1), jnp.float32),
            pltpu.VMEM((GROUPS, 1, ROWS), jnp.float32),
            pltpu.VMEM((GROUPS, GROUPS, ROWS), jnp.float32),
            pltpu.SemaphoreType.DMA((8,)),
            pltpu.SemaphoreType.DMA((len(STREAMS),)),
            pltpu.SemaphoreType.DMA((BINS, len(STREAMS))),
            pltpu.SemaphoreType.DMA((BINS, len(STREAMS))),
            pltpu.SemaphoreType.DMA((len(UNITS), 3)),
            pltpu.SemaphoreType.DMA((len(UNITS), 3)),
            pltpu.SemaphoreType.DMA((7, 2)),
            pltpu.SemaphoreType.DMA((7, 2)),
            pltpu.SemaphoreType.DMA((7,)),
            pltpu.SemaphoreType.DMA((7,)),
            pltpu.SemaphoreType.DMA((owners,)),
            pltpu.SemaphoreType.DMA((owners,)),
        ],
        compiler_params=pltpu.CompilerParams(
            collective_id=0, has_side_effects=True, vmem_limit_bytes=60 * 2**20
        ),
    )(
        origin.reshape(-1),
        meta,
        three_index.reshape(blocks * OB, NV, aux_local),
        meta,
        pair_screen,
        occupied_energy.T,
        virtual_energy.T,
    )
    return home.reshape(CHUNK, 2, 64)[: NV // SIDE, :, :NV].transpose(1, 0, 2)


def local(three_index, block_owner, pair_screen, orbital_counts, occupied_energy, virtual_energy):
    *spots, fits = plan(block_owner, orbital_counts)
    arguments = (
        three_index,
        block_owner,
        pair_screen,
        orbital_counts,
        occupied_energy,
        virtual_energy,
    )
    return lax.cond(
        fits,
        lambda: binned(*spots, *arguments),
        lambda: general(*arguments),
    )


def solution(mesh):
    in_specs = (P(None, None, ("grp", "aux")), P(), P(), P(), P(), P())
    out_specs = P("aux", "grp", None)
    return jax.shard_map(local, mesh=mesh, in_specs=in_specs, out_specs=out_specs, check_vma=False)
```

profile of v0, /device:TPU:1, one launch (start us, length us, event | category | flops | bytes accessed | tf_op | source)
XLA Modules:
  0.0 160.0 jit_solution(14077578966211247747)
XLA Ops:
  0.0 0.9 convert_reduce_fusion.1
  0.9 0.9 convert_reduce_fusion
  1.9 0.2 select_reduce_fusion.2
  2.0 0.7 broadcast_compare_fusion.2
  2.7 0.8 compare_and_fusion.2
  4.2 155.2 %conditional.1 = (f32[2,12,48]{2,0,1:T(2,128)S(1)}) conditional(s32[]{:T(128)} %convert_element_type.74, (s32[64]{0:T(128)}, bf16[64,768,128]{2,1,0:T(8,128)(2,1)}, f32[64,48]{0,1:T(8,128)}, f32[64,16]{0,1:T(8,128)}, s32[64]{0:T(128)}, /*index=5*/s32[64,64]{1,0:T(8,128)}) %tuple.31, (s32[64]{0:T(128)S(1)}, s32[64]{0:T(128)}, ...), branch_computations={%region_5.18_spmd, %region_17.21_spmd} | conditional | flops 4871736320 | bytes 219208608 | solution.py:830
  4.4 0.8 select_reduce_fusion.1
  5.2 0.7 fusion.3
  5.9 1.0 select_reduce_fusion
  6.9 0.1 copy.63
  6.9 0.7 reshape.481.origin_ref
  7.6 1.3 stack.23.meta_ref.meta
  8.9 149.4 %branch_1_fun.1 = f32[16,128]{1,0:T(8,128)} custom-call(s32[832]{0:T(1024)} %reshape.481.origin_ref, s32[8,64]{1,0:T(8,128)} %stack.23.meta_ref.meta, bf16[1024,48,128]{2,1,0:T(8,128)(2,1)} %bitcast.131, s32[8,64]{1,0:T(8,128)} %stack.23.meta_ref.meta, s32[64,64]{1,0:T(8,128)} %get-tuple-element.237.screen, f32[16,64]{1,0:T(8,128)} %bitcast.142, ...), custom_call_target="tpu_custom_call" | custom-call | tf_op jit(solution)/shard_map/cond/branch_1_fun/pallas_call | solution.py:766
  158.3 0.8 reshape.483
  159.4 0.0 copy-start.5
  159.4 0.6 copy-done.5
  (9 shorter events, 0.0 us)
Async XLA Ops:
  159.4 0.6 copy-start.5
where the time goes:
time: 160 us
  Pallas kernels  149 us (93%)
  other arithmetic  5.9 us (4%)
  local copies, waits for them, and re-layouts  3.39 us (2%)
    pallas_call x1, Pallas kernels, binned(): pl.pallas_call(kernel, out_shape=jax.ShapeDtypeStruct((CHUNK, 128), jnp.f...  149 us

commit v1 on v0

--- a/solution.py
+++ b/solution.py
@@ -291,7 +291,7 @@
     fold[...] = (
         lax.rem(lax.broadcasted_iota(jnp.int32, (ROWS, NV), 0), NV)
         == lax.broadcasted_iota(jnp.int32, (ROWS, NV), 1)
-    ).astype(jnp.float32)
+    ).astype(jnp.bfloat16)
     slot_sums[...] = jnp.zeros_like(slot_sums)
     row_sums[...] = jnp.zeros_like(row_sums)
     chunks[...] = jnp.zeros_like(chunks)
@@ -382,6 +382,16 @@
             preferred_element_type=jnp.float32,
         )
 
+    def fold_dot(left, axis=0):
+        total = 0.0
+        for _ in range(3):
+            piece = left.astype(jnp.bfloat16)
+            left = left - piece.astype(jnp.float32)
+            total = total + lax.dot_general(
+                piece, fold[...], (((1,), (axis,)), ((), ())), preferred_element_type=jnp.float32
+            )
+        return total
+
     blocks = meta.shape[1]
     slot_number = lax.broadcasted_iota(jnp.int32, (SLOTS, blocks), 0)
     orbital = slot_number - meta[1:2, :]
@@ -400,14 +410,18 @@
     order = jnp.where(row_slot < column_slot, 2.0, jnp.where(row_slot == column_slot, 1.0, 0.0))
     kind = jnp.where(live > 0.5, order, 0.0)
     for group in range(GROUPS):
-        lanes = exact_dot(energy[group * GROUP : (group + 1) * GROUP], fold[...], 1)
+        lanes = fold_dot(energy[group * GROUP : (group + 1) * GROUP], 1)
         lanes = jnp.sum(jnp.where(same_slot, lanes, 0.0), axis=0, keepdims=True)
         column_energy[group] = lanes
         row_energy[group] = jnp.sum(jnp.where(own_diagonal, lanes, 0.0), axis=1, keepdims=True)
         wide = lax.broadcasted_iota(jnp.int32, (SLOTS, ROWS), 0) == (
             group * GROUP + lax.broadcasted_iota(jnp.int32, (SLOTS, ROWS), 1) // NV
         )
-        mask[group] = exact_dot(kind, jnp.where(wide, 1.0, 0.0))
+        mask[group] = jnp.dot(
+            kind.astype(jnp.bfloat16),
+            jnp.where(wide, 1.0, 0.0).astype(jnp.bfloat16),
+            preferred_element_type=jnp.float32,
+        )
 
     def find(block, found):
         result = []
@@ -520,7 +534,7 @@
             def _():
                 diagonal = jnp.where(row_number == column_number, tile, 0.0)
                 diagonal = jnp.where(same_slot, jnp.sum(diagonal, axis=0, keepdims=True), 0.0)
-                diagonal = exact_dot(diagonal, fold[...])
+                diagonal = fold_dot(diagonal)
                 for part in range(8):
                     exact[column // 4, part, column % 4 : column % 4 + 1, :NV] = diagonal[
                         part : part + 1
@@ -542,7 +556,7 @@
         diagonal = exact[column // 4, own_part]
         for e in range(7):
             diagonal = diagonal + exact_parts[e, column // 4]
-        diagonal = exact_dot(diagonal[:, :NV], fold[...], 1)[column % 4 : column % 4 + 1]
+        diagonal = fold_dot(diagonal[:, :NV], 1)[column % 4 : column % 4 + 1]
 
         @pl.loop(0, v + 1)
         def _(u):
@@ -564,11 +578,8 @@
         product = lax.dot_general(
             stacked, stacked, (((0,), (0,)), ((), ())), preferred_element_type=jnp.float32
         )
-        slot_sums[(base + v) * ROWS : (base + v + 1) * ROWS, :] = jnp.dot(
-            jnp.where(row_number // NV == column_number // NV, product, 0.0),
-            fold[...],
-            precision=lax.Precision.HIGHEST,
-            preferred_element_type=jnp.float32,
+        slot_sums[(base + v) * ROWS : (base + v + 1) * ROWS, :] = fold_dot(
+            jnp.where(row_number // NV == column_number // NV, product, 0.0)
         )
 
     def advance(column, phase):
@@ -781,7 +792,7 @@
             pltpu.VMEM((PART_A * NV, ROWS), jnp.bfloat16),
             pltpu.VMEM((GROUPS, NV, NV), jnp.float32),
             pltpu.VMEM((SLOTS * NV, NV), jnp.float32),
-            pltpu.VMEM((ROWS, NV), jnp.float32),
+            pltpu.VMEM((ROWS, NV), jnp.bfloat16),
             pltpu.VMEM((8, 3 * CHUNK, 128), jnp.float32),
             pltpu.VMEM((7, 3 * CHUNK, 128), jnp.float32),
             pltpu.VMEM((owners, CHUNK, 128), jnp.float32),

time: 160 us -> 160 us (level)
  no operation moved by 1% of the time
where the time goes in v1:
time: 160 us
  Pallas kernels  149 us (93%)
  other arithmetic  5.9 us (4%)
  local copies, waits for them, and re-layouts  3.39 us (2%)
    pallas_call x1, Pallas kernels, binned(): pl.pallas_call(kernel, out_shape=jax.ShapeDtypeStruct((CHUNK, 128), jnp.f...  149 us

profile of v1, /device:TPU:1, one launch (start us, length us, event | category | flops | bytes accessed | tf_op | source)
XLA Modules:
  0.0 159.7 jit_solution(15100568242381761096)
XLA Ops:
  0.0 0.9 convert_reduce_fusion.1
  0.9 0.9 convert_reduce_fusion
  1.9 0.2 select_reduce_fusion.2
  2.0 0.7 broadcast_compare_fusion.2
  2.7 0.8 compare_and_fusion.2
  4.2 154.9 %conditional.1 = (f32[2,12,48]{2,0,1:T(2,128)S(1)}) conditional(s32[]{:T(128)} %convert_element_type.74, (s32[64]{0:T(128)}, bf16[64,768,128]{2,1,0:T(8,128)(2,1)}, f32[64,48]{0,1:T(8,128)}, f32[64,16]{0,1:T(8,128)}, s32[64]{0:T(128)}, /*index=5*/s32[64,64]{1,0:T(8,128)}) %tuple.31, (s32[64]{0:T(128)S(1)}, s32[64]{0:T(128)}, ...), branch_computations={%region_5.18_spmd, %region_17.21_spmd} | conditional | flops 4871736320 | bytes 219208608 | solution.py:841
  4.4 0.8 select_reduce_fusion.1
  5.2 0.7 fusion.3
  5.9 1.0 select_reduce_fusion
  6.9 0.1 copy.63
  6.9 0.7 reshape.481.origin_ref
  7.6 1.3 stack.23.meta_ref.meta
  8.9 149.2 %branch_1_fun.1 = f32[16,128]{1,0:T(8,128)} custom-call(s32[832]{0:T(1024)} %reshape.481.origin_ref, s32[8,64]{1,0:T(8,128)} %stack.23.meta_ref.meta, bf16[1024,48,128]{2,1,0:T(8,128)(2,1)} %bitcast.131, s32[8,64]{1,0:T(8,128)} %stack.23.meta_ref.meta, s32[64,64]{1,0:T(8,128)} %get-tuple-element.237.screen, f32[16,64]{1,0:T(8,128)} %bitcast.142, ...), custom_call_target="tpu_custom_call" | custom-call | tf_op jit(solution)/shard_map/cond/branch_1_fun/pallas_call | solution.py:777
  158.0 0.8 reshape.483
  159.1 0.0 copy-start.5
  159.1 0.6 copy-done.5
  (9 shorter events, 0.0 us)
Async XLA Ops:
  159.1 0.6 copy-start.5

commit v2 on v1

--- a/solution.py
+++ b/solution.py
@@ -118,7 +118,7 @@
     (48, 4, (0, 4)),
 )
 SENT = 52
-AHEAD = 2
+AHEAD = 1
 COLUMNS = tuple(
     [(0, v, v * (v + 1) // 2) for v in range(PART_A)]
     + [(PART_A, v, PART_A * (PART_A + 1) // 2 + v * (v + 1) // 2) for v in range(PART_B)]

time: 160 us -> 175 us (1.094)
  Pallas kernels: 149 us -> 164 us
    pallas_call x1, Pallas kernels: 149 us -> 164 us  [binned(): pl.pallas_call(kernel, out_shape=jax.ShapeDtypeStruct((CHUNK, 128), jnp.f...]
where the time goes in v2:
time: 175 us
  Pallas kernels  164 us (94%)
  other arithmetic  5.9 us (3%)
  local copies, waits for them, and re-layouts  3.39 us (2%)
    pallas_call x1, Pallas kernels, binned(): pl.pallas_call(kernel, out_shape=jax.ShapeDtypeStruct((CHUNK, 128), jnp.f...  164 us

profile of v2, /device:TPU:1, one launch (start us, length us, event | category | flops | bytes accessed | tf_op | source)
XLA Modules:
  0.0 175.0 jit_solution(4779471716480303106)
XLA Ops:
  0.0 0.9 convert_reduce_fusion.1
  0.9 0.9 convert_reduce_fusion
  1.9 0.2 select_reduce_fusion.2
  2.0 0.7 broadcast_compare_fusion.2
  2.7 0.8 compare_and_fusion.2
  4.2 170.2 %conditional.1 = (f32[2,12,48]{2,0,1:T(2,128)S(1)}) conditional(s32[]{:T(128)} %convert_element_type.74, (s32[64]{0:T(128)}, bf16[64,768,128]{2,1,0:T(8,128)(2,1)}, f32[64,48]{0,1:T(8,128)}, f32[64,16]{0,1:T(8,128)}, s32[64]{0:T(128)}, /*index=5*/s32[64,64]{1,0:T(8,128)}) %tuple.31, (s32[64]{0:T(128)S(1)}, s32[64]{0:T(128)}, ...), branch_computations={%region_5.18_spmd, %region_17.21_spmd} | conditional | flops 4871736320 | bytes 219208608 | solution.py:841
  4.4 0.8 select_reduce_fusion.1
  5.2 0.7 fusion.3
  5.9 1.0 select_reduce_fusion
  6.9 0.1 copy.63
  6.9 0.7 reshape.481.origin_ref
  7.6 1.3 stack.23.meta_ref.meta
  8.9 164.4 %branch_1_fun.1 = f32[16,128]{1,0:T(8,128)} custom-call(s32[832]{0:T(1024)} %reshape.481.origin_ref, s32[8,64]{1,0:T(8,128)} %stack.23.meta_ref.meta, bf16[1024,48,128]{2,1,0:T(8,128)(2,1)} %bitcast.131, s32[8,64]{1,0:T(8,128)} %stack.23.meta_ref.meta, s32[64,64]{1,0:T(8,128)} %get-tuple-element.237.screen, f32[16,64]{1,0:T(8,128)} %bitcast.142, ...), custom_call_target="tpu_custom_call" | custom-call | tf_op jit(solution)/shard_map/cond/branch_1_fun/pallas_call | solution.py:777
  173.3 0.8 reshape.483
  174.3 0.0 copy-start.5
  174.4 0.6 copy-done.5
  (9 shorter events, 0.0 us)
Async XLA Ops:
  174.3 0.6 copy-start.5
